TPU v7x, 256 devices: a whole 4x4x8 slice. The times are simulated.
256 devices in a mesh: row: 8 (over z), col: 16 (over x, y), vox: 2 (over core).
Axes of the slice: x: 4, y: 4, z: 8, core: 2. Of those that a mesh axis runs over, the one named last changes fastest.
Arguments:
- maps: bfloat16 [16384, 2048], P(('row', 'col'), 'vox'), may hold values from -21 to 21
- probes: bfloat16 [16384, 256], P(('row', 'col')), may hold values from -0.046875 to 0.046875
Outputs:
- gram: float32 [16384, 8, 16, 128], P('row', 'vox', 'col')
- basis: float32 [16384, 256], P(('row', 'col', 'vox'))
- factor: float32 [256, 256], replicated
All inputs are finite; a program needn't handle non-finite values.
Results may differ from a plain program's by a relative error of at most 0.004.
Values may be sent and summed in bfloat16 or wider, within the bound.
No kernel may reach another device: no remote copies, remote signals or barrier semaphores. Data moves between devices by JAX's collectives and lax.ppermute only.
A program may use at most 64 MiB of HBM per device.

v0:
```python
import jax
import jax.numpy as jnp
from jax import lax
from jax.sharding import PartitionSpec as P

VOX = 2048


def block_product(piece, partner):
    return (
        lax.dot_general(
            piece, partner, (((1,), (1,)), ((), ())), preferred_element_type=jnp.float32
        )
        / VOX
    )


def shards(maps, probes):
    sub_rows = maps.shape[0]
    row_count = lax.axis_size("row")
    col_count = lax.axis_size("col")
    vox_count = lax.axis_size("vox")
    subjects = sub_rows * row_count * col_count
    half_groups = row_count // vox_count
    vox_pos = lax.axis_index("vox")
    flat = maps.astype(jnp.float32)
    totals = lax.psum(jnp.sum(flat, axis=0), ("row", "col"))
    centered = (flat - totals[None, :] / subjects).astype(jnp.bfloat16)
    own_start = vox_pos * half_groups * sub_rows
    own_count = half_groups * sub_rows
    partial_sketch = None
    col_maps, col_probes = (
        lax.all_gather(centered, "row", axis=0, tiled=True),
        lax.all_gather(probes, "row", axis=0, tiled=True),
    )
    tile = block_product(lax.all_gather(centered, "col", axis=0, tiled=True), col_maps)
    block_rows = tile.shape[0]
    gram = lax.psum_scatter(
        tile.reshape(block_rows, row_count, 1, sub_rows), "vox", scatter_dimension=1, tiled=True
    )
    own_probes = lax.dynamic_slice_in_dim(col_probes, own_start, own_count, 0)
    partial_sketch = jnp.dot(
        gram.reshape(block_rows, own_count),
        own_probes.astype(jnp.float32),
        precision=lax.Precision.HIGHEST,
    )
    sketch = lax.psum_scatter(partial_sketch, ("col", "vox"), scatter_dimension=0, tiled=True)
    local_cross = lax.dot_general(
        sketch, sketch, (((0,), (0,)), ((), ())), precision=lax.Precision.HIGHEST
    )
    cross = lax.psum(local_cross, ("row", "col", "vox")) / subjects
    lower = jnp.linalg.cholesky(cross)
    basis = jax.scipy.linalg.solve_triangular(lower, sketch.T, lower=True).T
    return (gram, basis, lower.T)


def solution(mesh):
    placed = (P(("row", "col"), "vox"), P(("row", "col"), None))
    return jax.shard_map(
        shards,
        mesh=mesh,
        in_specs=placed,
        out_specs=(P("row", "vox", "col", None), P(("row", "col", "vox"), None), P()),
        check_vma=False,
    )
```

profile of v0, /device:TPU:2, one launch (start us, length us, event | category | flops | bytes accessed | tf_op | source)
XLA Modules:
  0.0 926.2 jit_solution(6317984655225748700)
XLA Ops:
  7.2 0.0 all-gather.5.cloned.1.call-start
  7.2 1.0 convert_reduce_fusion
  8.2 342.4 %psum.14 = f32[1024]{0:T(1024)S(1)} all-reduce(f32[1024]{0:T(1024)S(1)} %convert_reduce_fusion), channel_id=1, replica_groups=mesh['row'=8,'col'=16,'vox'=2] {'row','col'}, use_global_device_ids=true, to_apply=%region_1.0 | all-reduce | flops 1024 | bytes 8192 | tf_op jit(solution)/shard_map/psum | solution.py:27
  350.6 1.7 fusion
  352.3 0.0 all-gather.5.cloned.1.call-update
  352.3 0.0 all-gather.3.cloned.1.call-start
  352.4 0.7 all-gather.3.cloned.1.call-update
  353.1 0.0 reduce-scatter.3.cloned.1.call-start
  353.1 42.8 %all-gather.5.cloned.1.call-done = bf16[1024,1024]{1,0:T(8,128)(2,1)} async-done(((bf16[128,1024]{1,0:T(8,128)(2,1)}), bf16[1024,1024]{1,0:T(8,128)(2,1)}) %all-gather.5.cloned.1.call-update) | async-done | bytes 2097168 | tf_op jit(solution)/shard_map/all_gather | solution.py:33
  396.0 58.1 %all-gather.3.cloned.1.call-done = bf16[2048,1024]{1,0:T(8,128)(2,1)} async-done(((bf16[128,1024]{1,0:T(8,128)(2,1)}), bf16[2048,1024]{1,0:T(8,128)(2,1)}) %all-gather.3.cloned.1.call-update) | async-done | bytes 4194320 | tf_op jit(solution)/shard_map/all_gather | solution.py:36
  454.1 10.6 %convolution_multiply_fusion = f32[2048,1024]{0,1:T(8,128)} fusion(bf16[2048,1024]{1,0:T(8,128)(2,1)} %all-gather.3.cloned.1.call-done, bf16[1024,1024]{1,0:T(8,128)(2,1)} %all-gather.5.cloned.1.call-done), kind=kOutput, calls=%fused_computation.2 | convolution fusion | flops 4297064448 | bytes 14680064 | tf_op jit(solution)/shard_map/dot_general | solution.py:11
  464.7 9.1 copy.14
  473.8 0.0 copy-start.1
  473.8 0.0 reduce-scatter.3.cloned.1.call-update
  473.9 0.0 reduce-scatter.5.cloned.1.call-start
  473.9 0.8 copy-done.1
  474.7 26.8 %all_gather.11 = bf16[1024,256]{1,0:T(8,128)(2,1)S(1)} all-gather(bf16[128,256]{1,0:T(8,128)(2,1)S(1)} %copy-done.1), channel_id=1, replica_groups=mesh['row'=8,'col'=16,'vox'=2] {'row'}, dimensions={0}, use_global_device_ids=true | all-gather | bytes 589824 | tf_op jit(solution)/shard_map/all_gather | solution.py:34
  501.4 5.3 copy.15
  506.8 7.0 fusion.2
  513.7 0.0 reduce-scatter.5.cloned.1.call-update
  513.8 0.2 all-reduce.3.cloned.1.call-start
  514.0 84.6 %reduce-scatter.5.cloned.1.call-done = f32[64,256]{1,0:T(8,128)} async-done(((f32[2048,256]{1,0:T(8,128)}), f32[64,256]{1,0:T(8,128)}) %reduce-scatter.5.cloned.1.call-update) | async-done | bytes 65552 | tf_op jit(solution)/shard_map/reduce_scatter | solution.py:47
  598.6 2.0 fusion.15
  600.6 0.0 all-reduce.3.cloned.1.call-update
  600.6 8.4 copy.18
  609.1 246.4 %all-reduce.3.cloned.1.call-done = f32[256,256]{0,1:T(8,128)} async-done(((f32[256,256]{0,1:T(8,128)}), f32[256,256]{0,1:T(8,128)}) %all-reduce.3.cloned.1.call-update) | async-done | bytes 262160 | tf_op jit(solution)/shard_map/psum | solution.py:51
  855.5 1.0 broadcast_multiply_fusion
  856.4 0.1 copy.17
  856.6 1.0 fusion.1
  857.6 11.7 %cholesky.50 = f32[128,128]{1,0:T(8,128)S(1)} custom-call(f32[128,128]{1,0:T(8,128)S(1)} %cholesky.118), custom_call_target="Cholesky" | custom-call | tf_op jit(solution)/shard_map/jit(cholesky)/cholesky | solution.py:52
  869.3 9.8 %custom-call.15 = f32[1,128,128]{1,2,0:T(8,128)S(1)} custom-call(f32[1,128,128]{2,1,0:T(8,128)S(1)} %get-tuple-element.35), custom_call_target="InvertDiagBlocksLowerTriangular" | custom-call | tf_op jit(solution)/shard_map/jit(cholesky)/cholesky | solution.py:52
  879.1 0.2 constant_dynamic-update-slice_fusion.1
  879.4 0.3 convolution_subtract_fusion
  879.6 11.7 %cholesky.105 = f32[128,128]{1,0:T(8,128)S(1)} custom-call(f32[128,128]{1,0:T(8,128)S(1)} %convolution_subtract_fusion), custom_call_target="Cholesky" | custom-call | tf_op jit(solution)/shard_map/jit(cholesky)/cholesky | solution.py:52
  891.4 0.7 compare_reduce_fusion
  893.5 0.1 triangular_solve.57
  893.6 4.1 while.1
  893.6 0.6 fusion.26
  894.2 1.4 bitcast_dynamic-update-slice_fusion.2
  895.6 0.6 fusion.26
  896.2 1.4 bitcast_dynamic-update-slice_fusion.2
  897.7 19.9 %custom-call.16 = f32[2,128,128]{1,2,0:T(8,128)S(1)} custom-call(f32[2,128,128]{2,1,0:T(8,128)S(1)} %get-tuple-element.10), custom_call_target="InvertDiagBlocksLowerTriangular" | custom-call | tf_op jit(solution)/shard_map/jit(_solve_triangular)/triangular_solve | solution.py:53
  917.6 0.0 copy-done
  917.6 0.2 fusion.8
  917.8 0.2 convolution_subtract_fusion.1
  918.0 0.2 fusion.7
  918.2 0.6 maximum_bitcast_fusion
  918.8 0.8 copy.19
  (12 shorter events, 0.2 us)
Async XLA Ops:
  7.2 388.8 %all-gather.5.cloned.1.call-start = ((), (), s32[]{:S(2)}) async-start(), calls=%async_computation.3 | async-start | bytes 2359296 | tf_op jit(solution)/shard_map/all_gather | solution.py:33
  352.3 101.7 %all-gather.3.cloned.1.call-start = ((), (), s32[]{:S(2)}) async-start(), calls=%async_computation.2 | async-start | bytes 4456448 | tf_op jit(solution)/shard_map/all_gather | solution.py:36
  353.1 148.3 %reduce-scatter.3.cloned.1.call-start = ((), (), s32[]{:S(2)}) async-start(), calls=%async_computation.4 | async-start | bytes 12582912 | tf_op jit(solution)/shard_map/reduce_scatter | solution.py:38
  473.8 0.8 copy-start.1
  473.9 124.7 %reduce-scatter.5.cloned.1.call-start = ((), (), s32[]{:S(2)}) async-start(), calls=%async_computation.5 | async-start | bytes 2162688 | tf_op jit(solution)/shard_map/reduce_scatter | solution.py:47
  513.8 341.7 %all-reduce.3.cloned.1.call-start = ((), (), s32[]{:S(2)}) async-start(), calls=%async_computation.6 | async-start | bytes 524288 | tf_op jit(solution)/shard_map/psum | solution.py:51
  609.1 308.5 %copy-start = (f32[64,256]{1,0:T(8,128)S(1)}, f32[64,256]{1,0:T(8,128)}, u32[]{:S(2)}) copy-start(f32[64,256]{1,0:T(8,128)} %reduce-scatter.5.cloned.1.call-done) | copy-start | bytes 196612
Sparse Core Ops, SparseCore 0:
  352.5 43.4 all-gather.4
  399.0 55.0 all-gather.2
  474.0 21.9 reduce-scatter.2
  513.9 84.6 reduce-scatter.4
  605.3 250.0 all-reduce.2
where the time goes:
time: 927 us; the launch traced here: 926 us
  waiting for transfers between devices  433 us (47%)
  blocking collectives  369 us (40%)
  other arithmetic  59.3 us (6%)
  local copies, waits for them, and re-layouts  28.8 us (3%)
  matrix products  20.7 us (2%)
  between operations  15.2 us (2%)
    psum x1, blocking collectives, shards(): totals = lax.psum(jnp.sum(flat, axis=0), ('row', 'col'))  342 us
    psum x1, waiting for transfers between devices, shards(): cross = lax.psum(local_cross, ('row', 'col', 'vox')) / subjects  246 us
    reduce_scatter x1, waiting for transfers between devices, shards(): lax.psum_scatter(partial_sketch, ('col', 'vox'), scatter_dimension=0, til...  84.6 us
    all_gather x1, waiting for transfers between devices, shards(): lax.all_gather(centered, 'col', axis=0, tiled=True)  58.1 us
    all_gather x1, waiting for transfers between devices, shards(): lax.all_gather(centered, 'row', axis=0, tiled=True)  42.8 us
    another operation x6, other arithmetic, shards(): lower = jnp.linalg.cholesky(cross)  34 us
    all_gather x1, blocking collectives, shards(): lax.all_gather(probes, 'row', axis=0, tiled=True)  26.8 us
    another operation x2, other arithmetic, shards(): basis = jax.scipy.linalg.solve_triangular(lower, sketch.T, lower=True).T  19.9 us
  transfers between devices with their start and end apart: 5, of which 4 were waited for; matrix products, arithmetic and copies ran while one was open for 1% of the time, Pallas kernels for 0%

commit v1 on v0

--- a/solution.py
+++ b/solution.py
@@ -4,6 +4,14 @@
 from jax.sharding import PartitionSpec as P
 
 VOX = 2048
+
+
+def tiled_gather(array, axis, dim):
+    size = lax.axis_size(axis)
+    repeats = [size if d == dim else 1 for d in range(array.ndim)]
+    return lax.all_to_all(
+        jnp.tile(array, repeats), axis, split_axis=dim, concat_axis=dim, tiled=True
+    )
 
 
 def block_product(piece, partner):
@@ -33,7 +41,7 @@
         lax.all_gather(centered, "row", axis=0, tiled=True),
         lax.all_gather(probes, "row", axis=0, tiled=True),
     )
-    tile = block_product(lax.all_gather(centered, "col", axis=0, tiled=True), col_maps)
+    tile = block_product(tiled_gather(centered, "col", 0), col_maps)
     block_rows = tile.shape[0]
     gram = lax.psum_scatter(
         tile.reshape(block_rows, row_count, 1, sub_rows), "vox", scatter_dimension=1, tiled=True

time: 927 us -> 888 us (0.958)
  waiting for transfers between devices: 433 us -> 372 us
  starting transfers between devices: 0.38 us -> 15.5 us
    all_gather x1 -> x0, waiting for transfers between devices: 58.1 us -> none  [shards(): lax.all_gather(centered, 'col', axis=0, tiled=True)]
    all_to_all x0 -> x1, starting transfers between devices: none -> 15.1 us  [tiled_gather(): lax.all_to_all(jnp.tile(array, repeats), axis, split_axis=dim, concat_axi...]
  transfers between devices with their start and end apart: 5 -> 5, of which waited for: 4 -> 3; matrix products, arithmetic and copies ran while one was open for 1% -> 1% of each run, Pallas kernels for 0% -> 0%
where the time goes in v1:
time: 888 us; the launch traced here: 887 us
  blocking collectives  373 us (42%)
  waiting for transfers between devices  372 us (42%)
  other arithmetic  58.6 us (7%)
  local copies, waits for them, and re-layouts  31.3 us (4%)
  matrix products  20.7 us (2%)
  starting transfers between devices  15.5 us (2%)
  between operations  15.3 us (2%)
    psum x1, blocking collectives, shards(): totals = lax.psum(jnp.sum(flat, axis=0), ('row', 'col'))  348 us
    psum x1, waiting for transfers between devices, shards(): cross = lax.psum(local_cross, ('row', 'col', 'vox')) / subjects  246 us
    reduce_scatter x1, waiting for transfers between devices, shards(): lax.psum_scatter(partial_sketch, ('col', 'vox'), scatter_dimension=0, til...  84.6 us
    all_gather x1, waiting for transfers between devices, shards(): lax.all_gather(centered, 'row', axis=0, tiled=True)  40.5 us
    another operation x6, other arithmetic, shards(): lower = jnp.linalg.cholesky(cross)  34 us
    all_gather x1, blocking collectives, shards(): lax.all_gather(probes, 'row', axis=0, tiled=True)  25.5 us
    another operation x2, other arithmetic, shards(): basis = jax.scipy.linalg.solve_triangular(lower, sketch.T, lower=True).T  19.9 us
  transfers between devices with their start and end apart: 5, of which 3 were waited for; matrix products, arithmetic and copies ran while one was open for 1% of the time, Pallas kernels for 0%

profile of v1, /device:TPU:2, one launch (start us, length us, event | category | flops | bytes accessed | tf_op | source)
XLA Modules:
  0.0 886.8 jit_solution(3717286401033120403)
XLA Ops:
  7.2 1.0 convert_reduce_fusion
  8.2 347.7 %psum.14 = f32[1024]{0:T(1024)S(1)} all-reduce(f32[1024]{0:T(1024)S(1)} %convert_reduce_fusion), channel_id=1, replica_groups=mesh['row'=8,'col'=16,'vox'=2] {'row','col'}, use_global_device_ids=true, to_apply=%region_1.0 | all-reduce | flops 1024 | bytes 8192 | tf_op jit(solution)/shard_map/psum | solution.py:35
  355.9 1.0 fusion
  356.9 0.0 copy-start
  356.9 2.5 tile.2
  359.5 0.0 copy-done
  359.5 15.1 %all-to-all-start = ((bf16[16,128,1024]{2,1,0:T(8,128)(2,1)}), bf16[16,128,1024]{2,1,0:T(8,128)(2,1)}, u32[]{:S(2)}, u32[]{:S(2)}) async-start(bf16[16,128,1024]{2,1,0:T(8,128)(2,1)} %tile.2), calls=%async_computation | async-start | bytes 8388608 | tf_op jit(solution)/shard_map/all_to_all | solution.py:12
  374.6 0.0 all-gather.2.cloned.1.call-start
  374.6 0.7 all-gather.2.cloned.1.call-update
  375.3 0.0 reduce-scatter.3.cloned.1.call-start
  375.4 40.5 %all-gather.2.cloned.1.call-done = bf16[1024,1024]{1,0:T(8,128)(2,1)} async-done(((bf16[128,1024]{1,0:T(8,128)(2,1)}), bf16[1024,1024]{1,0:T(8,128)(2,1)}) %all-gather.2.cloned.1.call-update) | async-done | bytes 2097168 | tf_op jit(solution)/shard_map/all_gather | solution.py:41
  415.9 0.0 all-to-all-done
  415.9 10.6 %convolution_multiply_fusion = f32[2048,1024]{0,1:T(8,128)} fusion(bf16[2048,1024]{1,0:T(8,128)(2,1)} %bitcast, bf16[1024,1024]{1,0:T(8,128)(2,1)} %all-gather.2.cloned.1.call-done), kind=kOutput, calls=%fused_computation.2 | convolution fusion | flops 4297064448 | bytes 14680064 | tf_op jit(solution)/shard_map/dot_general | solution.py:19
  426.6 9.1 %copy.14 = f32[2048,8,1,128]{3,0,2,1:T(8,128)} copy(f32[2048,8,1,128]{0,3,1,2:T(8,128)} %bitcast.45) | data formatting | bytes 16777216 | tf_op jit(solution)/shard_map/reshape | solution.py:47
  435.7 0.0 reduce-scatter.3.cloned.1.call-update
  435.7 0.0 reduce-scatter.5.cloned.1.call-start
  435.8 0.8 copy-done.2
  436.5 25.5 %all_gather.7 = bf16[1024,256]{1,0:T(8,128)(2,1)S(1)} all-gather(bf16[128,256]{1,0:T(8,128)(2,1)S(1)} %copy-done.2), channel_id=1, replica_groups=mesh['row'=8,'col'=16,'vox'=2] {'row'}, dimensions={0}, use_global_device_ids=true | all-gather | bytes 589824 | tf_op jit(solution)/shard_map/all_gather | solution.py:42
  462.0 5.3 copy.15
  467.4 7.0 fusion.2
  474.3 0.0 reduce-scatter.5.cloned.1.call-update
  474.3 0.2 all-reduce.3.cloned.1.call-start
  474.6 84.6 %reduce-scatter.5.cloned.1.call-done = f32[64,256]{1,0:T(8,128)} async-done(((f32[2048,256]{1,0:T(8,128)}), f32[64,256]{1,0:T(8,128)}) %reduce-scatter.5.cloned.1.call-update) | async-done | bytes 65552 | tf_op jit(solution)/shard_map/reduce_scatter | solution.py:55
  559.2 2.0 fusion.15
  561.2 0.0 all-reduce.3.cloned.1.call-update
  561.3 8.4 copy.18
  569.7 246.3 %all-reduce.3.cloned.1.call-done = f32[256,256]{0,1:T(8,128)} async-done(((f32[256,256]{0,1:T(8,128)}), f32[256,256]{0,1:T(8,128)}) %all-reduce.3.cloned.1.call-update) | async-done | bytes 262160 | tf_op jit(solution)/shard_map/psum | solution.py:59
  816.0 1.0 broadcast_multiply_fusion
  817.0 0.1 copy.17
  817.1 1.0 fusion.1
  818.1 11.7 %cholesky.50 = f32[128,128]{1,0:T(8,128)S(1)} custom-call(f32[128,128]{1,0:T(8,128)S(1)} %cholesky.118), custom_call_target="Cholesky" | custom-call | tf_op jit(solution)/shard_map/jit(cholesky)/cholesky | solution.py:60
  829.9 9.8 %custom-call.15 = f32[1,128,128]{1,2,0:T(8,128)S(1)} custom-call(f32[1,128,128]{2,1,0:T(8,128)S(1)} %get-tuple-element.35), custom_call_target="InvertDiagBlocksLowerTriangular" | custom-call | tf_op jit(solution)/shard_map/jit(cholesky)/cholesky | solution.py:60
  839.7 0.2 constant_dynamic-update-slice_fusion.1
  839.9 0.3 convolution_subtract_fusion
  840.2 11.7 %cholesky.105 = f32[128,128]{1,0:T(8,128)S(1)} custom-call(f32[128,128]{1,0:T(8,128)S(1)} %convolution_subtract_fusion), custom_call_target="Cholesky" | custom-call | tf_op jit(solution)/shard_map/jit(cholesky)/cholesky | solution.py:60
  851.9 0.7 compare_reduce_fusion
  854.1 0.1 triangular_solve.57
  854.1 4.1 while.1
  854.1 0.6 fusion.26
  854.7 1.4 bitcast_dynamic-update-slice_fusion.2
  856.2 0.6 fusion.26
  856.8 1.4 bitcast_dynamic-update-slice_fusion.2
  858.2 19.9 %custom-call.16 = f32[2,128,128]{1,2,0:T(8,128)S(1)} custom-call(f32[2,128,128]{2,1,0:T(8,128)S(1)} %get-tuple-element.10), custom_call_target="InvertDiagBlocksLowerTriangular" | custom-call | tf_op jit(solution)/shard_map/jit(_solve_triangular)/triangular_solve | solution.py:61
  878.1 0.2 fusion.8
  878.3 0.2 convolution_subtract_fusion.1
  878.6 0.2 fusion.7
  878.8 0.6 maximum_bitcast_fusion
  879.4 0.8 copy.19
  (14 shorter events, 0.2 us)
Async XLA Ops:
  356.9 2.6 copy-start
  359.5 56.5 %all-to-all-start = ((bf16[16,128,1024]{2,1,0:T(8,128)(2,1)}), bf16[16,128,1024]{2,1,0:T(8,128)(2,1)}, u32[]{:S(2)}, u32[]{:S(2)}) async-start(bf16[16,128,1024]{2,1,0:T(8,128)(2,1)} %tile.2), calls=%async_computation | async-start | bytes 8388608 | tf_op jit(solution)/shard_map/all_to_all | solution.py:12
  374.6 41.3 %all-gather.2.cloned.1.call-start = ((), (), s32[]{:S(2)}) async-start(), calls=%async_computation.3 | async-start | bytes 2359296 | tf_op jit(solution)/shard_map/all_gather | solution.py:41
  375.3 86.7 %reduce-scatter.3.cloned.1.call-start = ((), (), s32[]{:S(2)}) async-start(), calls=%async_computation.4 | async-start | bytes 12582912 | tf_op jit(solution)/shard_map/reduce_scatter | solution.py:46
  435.7 0.8 copy-start.2
  435.7 123.5 %reduce-scatter.5.cloned.1.call-start = ((), (), s32[]{:S(2)}) async-start(), calls=%async_computation.5 | async-start | bytes 2162688 | tf_op jit(solution)/shard_map/reduce_scatter | solution.py:55
  474.3 341.7 %all-reduce.3.cloned.1.call-start = ((), (), s32[]{:S(2)}) async-start(), calls=%async_computation.6 | async-start | bytes 524288 | tf_op jit(solution)/shard_map/psum | solution.py:59
  569.7 308.4 %copy-start.1 = (f32[64,256]{1,0:T(8,128)S(1)}, f32[64,256]{1,0:T(8,128)}, u32[]{:S(2)}) copy-start(f32[64,256]{1,0:T(8,128)} %reduce-scatter.5.cloned.1.call-done) | copy-start | bytes 196612
Sparse Core Ops, SparseCore 0:
  377.8 38.0 all-gather.1
  435.8 20.8 reduce-scatter.2
  474.5 84.6 reduce-scatter.4
  566.0 250.0 all-reduce.2
